TPU v7x, 32 devices: a whole 2x2x4 slice. The times are simulated.
32 devices in a mesh: grp: 4 (over y, x), seq: 8 (over z, core).
Axes of the slice: x: 2, y: 2, z: 4, core: 2. Of those that a mesh axis runs over, the one named last changes fastest.
Arguments:
- passage_q: bfloat16 [16384, 4096], P(('grp', 'seq')), may hold values from -8 to 8
- passage_k: bfloat16 [16384, 512], P(('grp', 'seq')), may hold values from -8 to 8
- passage_v: bfloat16 [16384, 512], P(('grp', 'seq')), may hold values from -6 to 6
- kept: int32 [32, 4], P(('grp', 'seq')), may hold values from 0 to 1, as said below
- context_map: int32 [4, 8], P('grp', 'seq'), may hold values from 0 to 31, as said below
- recompute_pos: int32 [4, 512], P('grp', 'seq'), may hold values from 0 to 4095, as said below
- recompute_q: bfloat16 [4, 512, 4096], P('grp', 'seq'), may hold values from -8 to 8
- recompute_k: bfloat16 [4, 512, 512], P('grp', 'seq'), may hold values from -8 to 8
- recompute_v: bfloat16 [4, 512, 512], P('grp', 'seq'), may hold values from -6 to 6
Outputs:
- passage_out: bfloat16 [16384, 4096], P(('grp', 'seq'))
- reader_out: bfloat16 [4, 512, 4096], P('grp', 'seq')
Inputs may be any that keep to these rules, and one draw needn't show every extreme that they name: Block 0 of every passage is kept; a passage keeps at most 3 of its 4 blocks, and some passage keeps exactly 3. `context_map`: every passage appears exactly once. Entry [g, s] names a passage encoded on a device whose seq index is s. `recompute_pos`: entries [g, s * 64] to [g, (s + 1) * 64 - 1] are distinct ascending positions from s * 512 to (s + 1) * 512 - 1.
All inputs are finite; a program needn't handle non-finite values.
Results may differ from a plain program's by a relative error of at most 0.005.
Values may be sent and summed in bfloat16 or wider, within the bound.
A program may use at most 256 MiB of HBM per device.

v0:
```python
import jax
import jax.numpy as jnp
from jax import lax
from jax.sharding import PartitionSpec as P

HQ = 32
KVH = 4
HD = 128
PLEN = 512
BLK = 128
KEEP = 3
PASS_DEV = 1


far_position = 2**30


def encode_passage(queries, key_rows, value_rows):
    length = queries.shape[0]
    query_heads = queries.reshape(length, KVH, HQ // KVH, HD)
    key_heads = key_rows.reshape(length, KVH, HD)
    value_heads = value_rows.reshape(length, KVH, HD)
    scores = jnp.einsum(
        "ikgd,jkd->kgij", query_heads, key_heads, preferred_element_type=jnp.float32
    ) * HD ** (-0.5)
    causal = jnp.arange(length)[:, None] >= jnp.arange(length)[None, :]
    scores = jnp.where(causal, scores, -jnp.inf)
    maximum = jnp.max(scores, axis=-1, keepdims=True)
    weights = jnp.exp(scores - maximum).astype(jnp.bfloat16)
    totals = jnp.sum(weights, axis=-1, dtype=jnp.float32)
    mixture = jnp.einsum("kgij,jkd->ikgd", weights, value_heads, preferred_element_type=jnp.float32)
    mixture = mixture / jnp.moveaxis(totals, -1, 0)[..., None]
    return mixture.reshape(length, HQ * HD).astype(jnp.bfloat16)


def encode_items(items):
    return encode_passage(items[0], items[1], items[2])


def start_state(query_heads, own_keys, own_values):
    number = query_heads.shape[0]
    own_score = jnp.einsum(
        "rkgd,rkd->rkg",
        query_heads,
        own_keys.reshape(number, KVH, HD),
        preferred_element_type=jnp.float32,
    ) * HD ** (-0.5)
    totals = jnp.ones_like(own_score)
    mixture = jnp.broadcast_to(
        own_values.reshape(number, KVH, 1, HD).astype(jnp.float32), query_heads.shape
    )
    return (own_score, totals, mixture)


def block_length(number):
    length = number
    while length > 2048 and length % 2 == 0:
        length = length // 2
    return length


def absorb_keys(running, query_heads, query_pos, key_rows, value_rows, key_pos):
    number = key_rows.shape[0]
    length = block_length(number)
    blocks = number // length

    def visit_block(current, inputs):
        maximum, totals, mixture = current
        key_block, value_block, pos_block = inputs
        scores = jnp.einsum(
            "rkgd,nkd->rkgn",
            query_heads,
            key_block.reshape(length, KVH, HD),
            preferred_element_type=jnp.float32,
        ) * HD ** (-0.5)
        visible = pos_block[None, :] < query_pos[:, None]
        scores = jnp.where(visible[:, None, None, :], scores, -jnp.inf)
        new_maximum = jnp.maximum(maximum, jnp.max(scores, axis=-1))
        factor = jnp.exp(maximum - new_maximum)
        weights = jnp.exp(scores - new_maximum[..., None]).astype(jnp.bfloat16)
        totals = totals * factor + jnp.sum(weights, axis=-1, dtype=jnp.float32)
        mixture = mixture * factor[..., None] + jnp.einsum(
            "rkgn,nkd->rkgd",
            weights,
            value_block.reshape(length, KVH, HD),
            preferred_element_type=jnp.float32,
        )
        return ((new_maximum, totals, mixture), None)

    inputs = (
        key_rows.reshape(blocks, length, -1),
        value_rows.reshape(blocks, length, -1),
        key_pos.reshape(blocks, length),
    )
    running, ignored = lax.scan(visit_block, running, inputs)
    return running


def finish_state(running):
    maximum, totals, mixture = running
    return (mixture / totals[..., None]).reshape(mixture.shape[0], HQ * HD).astype(jnp.bfloat16)


def key_positions(block_ids, passage_rows):
    number = block_ids.shape[0]
    flat_rows = jnp.arange(number)
    shard_index = flat_rows // (PASS_DEV * passage_rows)
    within = flat_rows % (PASS_DEV * passage_rows)
    passage = within // passage_rows
    offset = within % BLK
    block_index = block_ids.astype(jnp.int32)
    position = (shard_index * PASS_DEV + passage) * PLEN + block_index * BLK + offset
    return jnp.where(block_index >= 0, position, far_position)


def on_device(
    passage_q,
    passage_k,
    passage_v,
    kept,
    context_map,
    recompute_pos,
    recompute_q,
    recompute_k,
    recompute_v,
):
    width_kv = passage_k.shape[1]
    block_count = PLEN // BLK
    items = (
        passage_q.reshape(PASS_DEV, PLEN, HQ * HD),
        passage_k.reshape(PASS_DEV, PLEN, width_kv),
        passage_v.reshape(PASS_DEV, PLEN, width_kv),
    )
    passage_out = lax.map(encode_items, items).reshape(PASS_DEV * PLEN, HQ * HD)
    split_keys = passage_k.reshape(PASS_DEV, block_count, BLK, width_kv)
    split_values = passage_v.reshape(PASS_DEV, block_count, BLK, width_kv)
    block_numbers = jnp.arange(block_count)
    ranking = jnp.cumsum(kept, axis=1) - 1
    slot_numbers = jnp.arange(KEEP)
    chosen = (kept[:, None, :] > 0) & (ranking[:, None, :] == slot_numbers[None, :, None])
    chosen_bf = chosen.astype(jnp.bfloat16)
    send_keys = jnp.einsum(
        "pkb,pbrc->pkrc", chosen_bf, split_keys, preferred_element_type=jnp.float32
    ).astype(jnp.bfloat16)
    send_values = jnp.einsum(
        "pkb,pbrc->pkrc", chosen_bf, split_values, preferred_element_type=jnp.float32
    ).astype(jnp.bfloat16)
    block_ids = jnp.sum(chosen.astype(jnp.int32) * (block_numbers + 1)[None, None, :], axis=-1) - 1
    kept_count = KEEP
    passage_rows = kept_count * BLK
    send_keys = send_keys.reshape(PASS_DEV, passage_rows, width_kv)
    send_values = send_values.reshape(PASS_DEV, passage_rows, width_kv)
    send_ids = jnp.repeat(block_ids, BLK, axis=1).astype(jnp.bfloat16)
    column = lax.axis_index("seq")
    seq_count = lax.axis_size("seq")
    wanted = context_map[0]
    piece_keys = lax.all_gather(send_keys, "grp", axis=0, tiled=True)
    piece_values = lax.all_gather(send_values, "grp", axis=0, tiled=True)
    piece_ids = lax.all_gather(send_ids, "grp", axis=0, tiled=True)
    number = piece_keys.shape[0]
    flat_rows = jnp.arange(number)
    passage_ids = (flat_rows // PASS_DEV * seq_count + column) * PASS_DEV + flat_rows % PASS_DEV
    picked = (wanted[:, None] == passage_ids[None, :]).astype(jnp.bfloat16)
    local_keys = (
        jnp.einsum("tm,mlc->tlc", picked, piece_keys, preferred_element_type=jnp.float32)
        .astype(jnp.bfloat16)
        .reshape(PASS_DEV * passage_rows, width_kv)
    )
    local_values = (
        jnp.einsum("tm,mlc->tlc", picked, piece_values, preferred_element_type=jnp.float32)
        .astype(jnp.bfloat16)
        .reshape(PASS_DEV * passage_rows, width_kv)
    )
    local_ids = (
        jnp.einsum("tm,ml->tl", picked, piece_ids, preferred_element_type=jnp.float32)
        .astype(jnp.bfloat16)
        .reshape(PASS_DEV * passage_rows)
    )
    query_rows = recompute_q[0]
    own_keys = recompute_k[0]
    own_values = recompute_v[0]
    query_pos = recompute_pos[0]
    recompute_count = query_rows.shape[0]
    query_heads = query_rows.reshape(recompute_count, KVH, HQ // KVH, HD)
    running = start_state(query_heads, own_keys, own_values)
    last_query = jnp.max(query_pos)
    pieces = (
        lax.all_gather(local_keys, "seq", axis=0, tiled=True),
        lax.all_gather(local_values, "seq", axis=0, tiled=True),
        lax.all_gather(local_ids, "seq", axis=0, tiled=True),
    )
    piece_pos = key_positions(pieces[2], passage_rows)
    needed = jnp.min(piece_pos) < last_query
    running = lax.cond(
        needed,
        lambda state_now: absorb_keys(
            state_now, query_heads, query_pos, pieces[0], pieces[1], piece_pos
        ),
        lambda state_now: state_now,
        running,
    )
    reader_rows = finish_state(running)
    return (passage_out, reader_rows[None])


def solution(mesh):
    return jax.shard_map(
        on_device,
        mesh=mesh,
        in_specs=(
            P(("grp", "seq"), None),
            P(("grp", "seq"), None),
            P(("grp", "seq"), None),
            P(("grp", "seq"), None),
            P("grp", "seq"),
            P("grp", "seq"),
            P("grp", "seq", None),
            P("grp", "seq", None),
            P("grp", "seq", None),
        ),
        out_specs=(P(("grp", "seq"), None), P("grp", "seq", None)),
        check_vma=False,
    )
```

profile of v0, /device:TPU:25, one launch (start us, length us, event | category | flops | bytes accessed | tf_op | source)
XLA Modules:
  0.0 215.8 jit_solution(11407815116552982710)
XLA Ops:
  14.3 29.0 %all-gather.7.cloned.1.call-done = bf16[4,384,512]{2,1,0:T(8,128)(2,1)} async-done(((bf16[1,384,512]{2,1,0:T(8,128)(2,1)}), bf16[4,384,512]{2,1,0:T(8,128)(2,1)}) %all-gather.7.cloned.1.call-update) | async-done | bytes 1572880 | tf_op jit(solution)/shard_map/all_gather | solution.py:157
  43.2 2.7 %fusion.11 = bf16[1,384,512]{2,0,1:T(2,128)(2,1)S(1)} fusion(bf16[4,384,512]{2,1,0:T(8,128)(2,1)} %all-gather.7.cloned.1.call-done, s32[]{:T(128)S(6)} %axis_index.12, s32[]{:T(128)} %bitcast.118), kind=kOutput, calls=%fused_computation.26 | convolution fusion | flops 1572876 | bytes 1966088 | tf_op jit(solution)/shard_map/tm,mlc->tlc/dot_general | solution.py:165
  49.4 3.4 %copy.103 = bf16[64,8,32,128]{3,2,1,0:T(8,128)(2,1)S(1)} copy(bf16[64,8,32,128]{3,1,2,0:T(8,128)(2,1)} %bitcast.124) | data formatting | bytes 8388608
  53.0 14.4 %fusion.5 = (f32[4,8,512]{2,1,0:T(8,128)S(1)}, f32[4,512,512,8]{2,1,3,0:T(8,128)}) fusion(pred[512,512]{0,1:T(8,128)(4,1)S(1)} %iota_compare_fusion, bf16[512,4,8,128]{3,2,1,0:T(8,128)(2,1)S(1)} %bitcast.123, bf16[512,4,128,1]{2,1,0,3:T(4,128)(2,1)S(1)} %bitcast.126), kind=kOutput, calls=%fused_computation.19 | convolution fusion | flops 2172633088 | bytes 38600704 | tf_op jit(solution)/shard_map/while/body/eval_jaxpr/ikgd,jkd->kgij/dot_general | solution.py:23
  67.3 9.3 %all-gather.11.cloned.1.call-done = bf16[4,384,512]{2,1,0:T(8,128)(2,1)} async-done(((bf16[1,384,512]{2,1,0:T(8,128)(2,1)}), bf16[4,384,512]{2,1,0:T(8,128)(2,1)}) %all-gather.11.cloned.1.call-update) | async-done | bytes 1572880 | tf_op jit(solution)/shard_map/all_gather | solution.py:158
  76.6 2.7 %fusion.9 = bf16[1,384,512]{2,0,1:T(2,128)(2,1)S(1)} fusion(bf16[4,384,512]{2,1,0:T(8,128)(2,1)} %all-gather.11.cloned.1.call-done, s32[]{:T(128)S(6)} %axis_index.12, s32[]{:T(128)} %bitcast.117), kind=kOutput, calls=%fused_computation.24 | convolution fusion | flops 1572876 | bytes 1966088 | tf_op jit(solution)/shard_map/tm,mlc->tlc/dot_general | solution.py:170
  80.2 14.7 %convert_reduce_fusion.1 = f32[4,8,512]{2,1,0:T(8,128)S(1)} fusion(f32[4,8,512]{2,1,0:T(8,128)S(1)} %get-tuple-element.215, f32[4,512,512,8]{2,1,3,0:T(8,128)} %get-tuple-element.216, pred[512,512]{0,1:T(8,128)(4,1)S(1)} %iota_compare_fusion), kind=kLoop, calls=%fused_computation.17 | loop fusion | flops 50315264 | bytes 33947648 | tf_op jit(solution)/shard_map/while/body/eval_jaxpr/reduce_sum | solution.py:30
  94.9 16.6 %fusion.6 = bf16[512,4,8,128]{0,3,2,1:T(8,128)(2,1)} fusion(f32[512,4,8]{0,2,1:T(8,128)S(1)} %bitcast.137, bf16[512,4,128,1]{0,2,3,1:T(8,128)(2,1)S(1)} %bitcast.136, f32[4,512,512,8]{2,1,3,0:T(8,128)} %get-tuple-element.216, f32[4,8,512]{2,1,0:T(8,128)S(1)} %get-tuple-element.215, pred[512,512]{0,1:T(8,128)(4,1)S(1)} %iota_compare_fusion), kind=kOutput, calls=%fused_computation.21 | convolution fusion | flops 2185232384 | bytes 38666240 | tf_op jit(solution)/shard_map/while/body/eval_jaxpr/kgij,jkd->ikgd/dot_general | solution.py:31
  111.5 6.3 %copy.81 = bf16[512,4096]{1,0:T(8,128)(2,1)} copy(bf16[512,4096]{0,1:T(8,128)(2,1)} %bitcast.125) | data formatting | bytes 8388608
  118.1 6.0 %all-gather = bf16[4,1,384]{2,1,0:T(2,128)(2,1)S(1)} all-gather(bf16[1,1,384]{2,1,0:T(2,128)(2,1)S(1)} %reshape.340), channel_id=1, replica_groups=mesh['grp'=4,'seq'=8] {'grp'}, dimensions={0}, use_global_device_ids=true | all-gather | bytes 3840 | tf_op jit(solution)/shard_map/all_gather | solution.py:159
  124.2 14.6 %all-gather.1 = bf16[8,1,384]{2,1,0:T(2,128)(2,1)S(1)} all-gather(bf16[1,1,384]{2,1,0:T(2,128)(2,1)S(1)} %reshape.342), channel_id=1, replica_groups=mesh['grp'=4,'seq'=8] {'seq'}, dimensions={0}, use_global_device_ids=true | all-gather | bytes 6912 | tf_op jit(solution)/shard_map/all_gather | solution.py:190
  142.3 12.1 %all-gather.13.cloned.1.call-done = bf16[3072,512]{1,0:T(8,128)(2,1)} async-done(((bf16[384,512]{1,0:T(8,128)(2,1)}), bf16[3072,512]{1,0:T(8,128)(2,1)}) %all-gather.13.cloned.1.call-update) | async-done | bytes 3145744 | tf_op jit(solution)/shard_map/all_gather | solution.py:189
  155.5 50.8 %conditional.1 = (f32[64,4,8]{0,2,1:T(8,128)}, f32[64,4,8,128]{3,0,2,1:T(8,128)}) conditional(s32[]{:T(128)} %convert_element_type.98, f32[64,4,8,128]{3,0,2,1:T(8,128)} %broadcast_in_dim.70, (f32[64,4,8]{0,2,1:T(8,128)S(1)}, bf16[3072,512]{1,0:T(8,128)(2,1)}, bf16[3072,512]{1,0:T(8,128)(2,1)}, s32[3072]{0:T(1024)S(1)}, s32[1,64]{1,0:T(1,128)S(1)}, ...), branch_computations={%region_6.7_spmd, %region_7.12_spmd} | conditional | flops 1652137984 | bytes 108063248 | solution.py:194
  156.5 49.8 %while.4 = (s32[]{:T(128)}, f32[64,4,8]{0,2,1:T(8,128)S(1)}, f32[64,4,8]{0,2,1:T(8,128)}, f32[64,4,8,128]{3,0,2,1:T(8,128)}, s32[2,1536]{1,0:T(2,128)S(1)}, /*in...) while((s32[]{:T(128)}, f32[64,4,8]{0,2,1:T(8,128)S(1)}, ...), condition=%wide.region_11.11_spmd.clone, body=%wide.region_8.10_spmd.clone.sunk | while | flops 1652135936 | bytes 106973600 | solution.py:95
  156.7 3.2 %constant_dynamic-slice_fusion.3 = (bf16[1,1536,512]{2,1,0:T(8,128)(2,1)S(1)}, bf16[1,1536,512]{2,1,0:T(8,128)(2,1)}) fusion(bf16[2,1536,512]{2,1,0:T(8,128)(2,1)} %get-tuple-element.314, s32[]{:T(128)S(6)} %copy.135, bf16[2,1536,512]{2,1,0:T(8,128)(2,1)} %get-tuple-element.312), kind=kLoop, calls=%fused_computation.11.clone.1 | loop fusion | bytes 6291460 | tf_op jit(solution)/shard_map/cond/branch_1_fun/while/body/jit(dynamic_index_in_dim)/dynamic_slice | solution.py:95
  161.7 3.1 %fusion.63 = (f32[64,4,8]{0,2,1:T(8,128)S(1)}, f32[4,1536,64,8]{1,2,3,0:T(8,128)S(1)}) fusion(pred[64,1536]{1,0:T(8,128)(4,1)S(1)} %broadcast_compare_fusion.2, bf16[1536,4,128,1]{0,2,3,1:T(8,128)(2,1)S(1)} %bitcast.119, bf16[64,4,8,128]{3,0,2,1:T(8,128)(2,1)} %get-tuple-element.313), kind=kOutput, calls=%fused_computation.3.clone.1 | convolution fusion | flops 814741504 | bytes 14786560 | tf_op jit(solution)/shard_map/cond/branch_1_fun/while/body/eval_jaxpr/rkgd,nkd->rkgn/dot_general | solution.py:70
  164.7 4.6 %copy-done = f32[4,1536,64,8]{1,2,3,0:T(8,128)} copy-done((f32[4,1536,64,8]{1,2,3,0:T(8,128)}, f32[4,1536,64,8]{1,2,3,0:T(8,128)S(1)}, u32[]{:S(2)}) %copy-start) | copy-done | bytes 12582936 | tf_op jit(solution)/shard_map/cond/branch_1_fun/while
  169.3 3.2 %convert_reduce_fusion.3 = f32[64,4,8]{0,2,1:T(8,128)S(1)} fusion(f32[64,4,8]{0,2,1:T(8,128)S(1)} %max.5, f32[4,1536,64,8]{1,2,3,0:T(8,128)S(1)} %get-tuple-element.280, pred[64,1536]{1,0:T(8,128)(4,1)S(1)} %broadcast_compare_fusion.2), kind=kLoop, calls=%fused_computation.1.clone.1 | loop fusion | flops 18872320 | bytes 12697600 | tf_op jit(solution)/shard_map/cond/branch_1_fun/while/body/eval_jaxpr/reduce_sum | solution.py:81
  173.9 7.2 %fusion.65 = f32[64,4,8,128]{3,0,2,1:T(8,128)} fusion(bf16[1536,4,128,1]{0,2,3,1:T(8,128)(2,1)S(1)} %bitcast.120, f32[64,4,8,128]{3,0,2,1:T(8,128)} %get-tuple-element.298, f32[64,4,8]{0,2,1:T(8,128)S(1)} %get-tuple-element.283, f32[4,1536,64,8]{1,2,3,0:T(8,128)} %copy-done, f32[64,4,8]{0,2,1:T(8,128)S(1)} %max.5, ...), kind=kOutput, calls=%fused_computation.5.clone.1 | convolution fusion | flops 818413568 | bytes 16367616 | tf_op jit(solution)/shard_map/cond/branch_1_fun/while/body/eval_jaxpr/rkgn,nkd->rkgd/dot_general | solution.py:82
  181.2 3.2 %constant_dynamic-slice_fusion.3 = (bf16[1,1536,512]{2,1,0:T(8,128)(2,1)S(1)}, bf16[1,1536,512]{2,1,0:T(8,128)(2,1)}) fusion(bf16[2,1536,512]{2,1,0:T(8,128)(2,1)} %get-tuple-element.314, s32[]{:T(128)S(6)} %copy.135, bf16[2,1536,512]{2,1,0:T(8,128)(2,1)} %get-tuple-element.312), kind=kLoop, calls=%fused_computation.11.clone.1 | loop fusion | bytes 6291460 | tf_op jit(solution)/shard_map/cond/branch_1_fun/while/body/jit(dynamic_index_in_dim)/dynamic_slice | solution.py:95
  186.2 3.1 %fusion.63 = (f32[64,4,8]{0,2,1:T(8,128)S(1)}, f32[4,1536,64,8]{1,2,3,0:T(8,128)S(1)}) fusion(pred[64,1536]{1,0:T(8,128)(4,1)S(1)} %broadcast_compare_fusion.2, bf16[1536,4,128,1]{0,2,3,1:T(8,128)(2,1)S(1)} %bitcast.119, bf16[64,4,8,128]{3,0,2,1:T(8,128)(2,1)} %get-tuple-element.313), kind=kOutput, calls=%fused_computation.3.clone.1 | convolution fusion | flops 814741504 | bytes 14786560 | tf_op jit(solution)/shard_map/cond/branch_1_fun/while/body/eval_jaxpr/rkgd,nkd->rkgn/dot_general | solution.py:70
  189.3 4.6 %copy-done = f32[4,1536,64,8]{1,2,3,0:T(8,128)} copy-done((f32[4,1536,64,8]{1,2,3,0:T(8,128)}, f32[4,1536,64,8]{1,2,3,0:T(8,128)S(1)}, u32[]{:S(2)}) %copy-start) | copy-done | bytes 12582936 | tf_op jit(solution)/shard_map/cond/branch_1_fun/while
  193.8 3.2 %convert_reduce_fusion.3 = f32[64,4,8]{0,2,1:T(8,128)S(1)} fusion(f32[64,4,8]{0,2,1:T(8,128)S(1)} %max.5, f32[4,1536,64,8]{1,2,3,0:T(8,128)S(1)} %get-tuple-element.280, pred[64,1536]{1,0:T(8,128)(4,1)S(1)} %broadcast_compare_fusion.2), kind=kLoop, calls=%fused_computation.1.clone.1 | loop fusion | flops 18872320 | bytes 12697600 | tf_op jit(solution)/shard_map/cond/branch_1_fun/while/body/eval_jaxpr/reduce_sum | solution.py:81
  199.1 7.2 %fusion.65 = f32[64,4,8,128]{3,0,2,1:T(8,128)} fusion(bf16[1536,4,128,1]{0,2,3,1:T(8,128)(2,1)S(1)} %bitcast.120, f32[64,4,8,128]{3,0,2,1:T(8,128)} %get-tuple-element.298, f32[64,4,8]{0,2,1:T(8,128)S(1)} %get-tuple-element.283, f32[4,1536,64,8]{1,2,3,0:T(8,128)} %copy-done, f32[64,4,8]{0,2,1:T(8,128)S(1)} %max.5, ...), kind=kOutput, calls=%fused_computation.5.clone.1 | convolution fusion | flops 818413568 | bytes 16367616 | tf_op jit(solution)/shard_map/cond/branch_1_fun/while/body/eval_jaxpr/rkgn,nkd->rkgd/dot_general | solution.py:82
  (71 shorter events, 25.5 us)
Async XLA Ops:
  7.2 36.1 %all-gather.7.cloned.1.call-start = ((), (), s32[]{:S(2)}) async-start(), calls=%async_computation | async-start | bytes 1966080 | tf_op jit(solution)/shard_map/all_gather | solution.py:157
  11.1 65.5 %all-gather.11.cloned.1.call-start = ((), (), s32[]{:S(2)}) async-start(), calls=%async_computation.2 | async-start | bytes 1966080 | tf_op jit(solution)/shard_map/all_gather | solution.py:158
  13.6 128.7 %all-gather.9.cloned.1.call-start = ((), (), s32[]{:S(2)}) async-start(), calls=%async_computation.1 | async-start | bytes 3538944 | tf_op jit(solution)/shard_map/all_gather | solution.py:188
  46.8 107.6 %all-gather.13.cloned.1.call-start = ((), (), s32[]{:S(2)}) async-start(), calls=%async_computation.3 | async-start | bytes 3538944 | tf_op jit(solution)/shard_map/all_gather | solution.py:189
  94.9 44.0 %copy-start.4 = (s32[1,64]{1,0:T(1,128)S(1)}, s32[1,64]{1,0:T(1,128)}, u32[]{:S(2)}) copy-start(s32[1,64]{1,0:T(1,128)} %param.18) | copy-start | bytes 772
  94.9 46.7 %copy-start.2 = (bf16[1,64,512]{2,1,0:T(8,128)(2,1)S(1)}, bf16[1,64,512]{2,1,0:T(8,128)(2,1)}, u32[]{:S(2)}) copy-start(bf16[1,64,512]{2,1,0:T(8,128)(2,1)} %param.21) | copy-start | bytes 196612
  94.9 46.7 %copy-start.1 = (bf16[1,64,4096]{2,1,0:T(8,128)(2,1)S(1)}, bf16[1,64,4096]{2,1,0:T(8,128)(2,1)}, u32[]{:S(2)}) copy-start(bf16[1,64,4096]{2,1,0:T(8,128)(2,1)} %param.19) | copy-start | bytes 1572868
  94.9 46.8 %copy-start.3 = (bf16[1,64,512]{2,1,0:T(8,128)(2,1)S(1)}, bf16[1,64,512]{2,1,0:T(8,128)(2,1)}, u32[]{:S(2)}) copy-start(bf16[1,64,512]{2,1,0:T(8,128)(2,1)} %param.20) | copy-start | bytes 196612
  164.7 4.6 %copy-start = (f32[4,1536,64,8]{1,2,3,0:T(8,128)}, f32[4,1536,64,8]{1,2,3,0:T(8,128)S(1)}, u32[]{:S(2)}) copy-start(f32[4,1536,64,8]{1,2,3,0:T(8,128)S(1)} %get-tuple-element.280) | copy-start | bytes 37748740 | tf_op jit(solution)/shard_map/cond/branch_1_fun/while
  189.2 4.6 %copy-start = (f32[4,1536,64,8]{1,2,3,0:T(8,128)}, f32[4,1536,64,8]{1,2,3,0:T(8,128)S(1)}, u32[]{:S(2)}) copy-start(f32[4,1536,64,8]{1,2,3,0:T(8,128)S(1)} %get-tuple-element.280) | copy-start | bytes 37748740 | tf_op jit(solution)/shard_map/cond/branch_1_fun/while
Sparse Core Ops, SparseCore 0:
  11.2 31.9 all-gather.6
  45.6 30.9 all-gather.10
  78.9 36.6 all-gather.8
  117.1 37.2 all-gather.12
where the time goes:
time: 220 us; the launch traced here: 216 us
  matrix products  60.5 us (28%)
  waiting for transfers between devices  50.4 us (23%)
  local copies, waits for them, and re-layouts  39.8 us (18%)
  other arithmetic  28.1 us (13%)
  blocking collectives  20.6 us (9%)
  between operations  15.9 us (7%)
    all_gather x1, waiting for transfers between devices, on_device(): piece_keys = lax.all_gather(send_keys, 'grp', axis=0, tiled=True)  29 us
    dot_general x1, matrix products, encode_passage(): jnp.einsum('kgij,jkd->ikgd', weights, value_heads, preferred_element_type...  16.6 us
    reduce_sum x1, other arithmetic, encode_passage(): totals = jnp.sum(weights, axis=-1, dtype=jnp.float32)  14.7 us
    all_gather x1, blocking collectives, on_device(): lax.all_gather(local_ids, 'seq', axis=0, tiled=True)  14.6 us
    dot_general x2, matrix products, visit_block(): jnp.einsum('rkgn,nkd->rkgd', weights, value_block.reshape(length, KVH, HD...  14.4 us
    dot_general x1, matrix products, encode_passage(): jnp.einsum('ikgd,jkd->kgij', query_heads, key_heads, preferred_element_ty...  14.4 us
    all_gather x1, waiting for transfers between devices, on_device(): lax.all_gather(local_values, 'seq', axis=0, tiled=True)  12.1 us
    dynamic_slice x8, local copies, waits for them, and re-layouts, absorb_keys(): running, ignored = lax.scan(visit_block, running, inputs)  11.4 us
  transfers between devices with their start and end apart: 4, of which 3 were waited for; matrix products, arithmetic and copies ran while one was open for 32% of the time, Pallas kernels for 0%

commit v1 on v0

v1 whole, which is shorter than its diff:
```python
import functools
import math

import jax
import jax.numpy as jnp
from jax import lax
from jax.experimental import pallas as pl
from jax.experimental.pallas import tpu as pltpu
from jax.sharding import PartitionSpec as P

HQ = 32
KVH = 4
HD = 128
PLEN = 512
BLK = 128
KEEP = 3
NBLK = PLEN // BLK
ROWS = KEEP * BLK
GQ = HQ // KVH
WKV = KVH * HD
QB = 256
SCALE2 = HD ** (-0.5) * math.log2(math.e)
NEG = -1e30


def dot_nt(a, b):
    return lax.dot_general(a, b, (((1,), (1,)), ((), ())), preferred_element_type=jnp.float32)


def with_ones(values):
    return jnp.concatenate([values, jnp.ones_like(values)], axis=1)


def passage_head(queries, keys, values_ones, first):
    number = first + QB
    scores = dot_nt(queries, keys[:number])
    row = lax.broadcasted_iota(jnp.int32, (QB, QB), 0)
    col = lax.broadcasted_iota(jnp.int32, (QB, QB), 1)
    diagonal = jnp.where(row >= col, scores[:, first:], NEG)
    scores = diagonal if first == 0 else jnp.concatenate([scores[:, :first], diagonal], axis=1)
    maximum = jnp.max(scores, axis=-1, keepdims=True)
    weights = jnp.exp2((scores - maximum) * SCALE2).astype(jnp.bfloat16)
    mixture = jnp.dot(weights, values_ones[:number], preferred_element_type=jnp.float32)
    return (mixture[:, :HD] / mixture[:, HD:]).astype(jnp.bfloat16)


def passage_kernel(q_ref, k_ref, v_ref, out_ref):
    keys = k_ref[...]
    values_ones = with_ones(v_ref[...])
    for head in range(GQ):
        cols = slice(head * HD, (head + 1) * HD)
        for first in range(0, PLEN, QB):
            rows = slice(first, first + QB)
            out_ref[rows, cols] = passage_head(q_ref[rows, cols], keys, values_ones, first)


def reader_kernel(q_ref, ok_ref, ov_ref, bias_ref, k_ref, v_ref, out_ref, m_ref, acc_ref):
    count = q_ref.shape[0]
    me = lax.axis_index("seq")
    own_k = ok_ref[...].astype(jnp.float32)
    own_v = ov_ref[...].astype(jnp.float32)
    queries = jnp.concatenate(
        [q_ref[:, h * HD : (h + 1) * HD] for h in range(GQ)], axis=0
    )
    own_tiled = jnp.concatenate([own_k] * GQ, axis=0)
    own_score = jnp.sum(queries.astype(jnp.float32) * own_tiled, axis=-1, keepdims=True)
    m_ref[...] = jnp.broadcast_to(own_score, m_ref.shape)
    acc_ref[:, :HD] = jnp.concatenate([own_v] * GQ, axis=0)
    acc_ref[:, HD:] = jnp.ones((GQ * count, HD), jnp.float32)

    def shard(index, carry):
        scores = dot_nt(queries, k_ref[index])
        bias = bias_ref[index]
        scores = scores + jnp.concatenate([bias] * GQ, axis=0)
        old = m_ref[...]
        new = jnp.maximum(old, jnp.max(scores, axis=-1, keepdims=True))
        factor = jnp.exp2((old - new) * SCALE2)
        weights = jnp.exp2(
            (scores - jnp.concatenate([new] * KEEP, axis=1)) * SCALE2
        ).astype(jnp.bfloat16)
        mixture = jnp.dot(weights, with_ones(v_ref[index]), preferred_element_type=jnp.float32)
        acc_ref[...] = acc_ref[...] * jnp.concatenate([factor, factor], axis=1) + mixture
        m_ref[...] = new
        return carry

    lax.fori_loop(0, me + 1, shard, 0)
    result = (acc_ref[:, :HD] / acc_ref[:, HD:]).astype(out_ref.dtype)
    for h in range(GQ):
        out_ref[:, h * HD : (h + 1) * HD] = result[h * count : (h + 1) * count]


def on_device(passage_q, passage_k, passage_v, kept, context_map, recompute_pos,
              recompute_q, recompute_k, recompute_v):
    groups = lax.axis_size("grp")
    seqs = lax.axis_size("seq")
    count = recompute_q.shape[1]
    group = lax.axis_index("grp")
    column = lax.axis_index("seq")

    info = jnp.concatenate([kept, context_map], axis=1)
    everyone = lax.all_gather(info, ("grp", "seq"), axis=0, tiled=True)
    all_kept = everyone[:, :NBLK]
    my_map = lax.dynamic_slice_in_dim(everyone[:, NBLK], group * seqs, seqs)

    def block_ids(flags):
        ranking = jnp.cumsum(flags, axis=-1) - 1
        slots = jnp.arange(KEEP)
        chosen = (flags[..., None, :] > 0) & (ranking[..., None, :] == slots[:, None])
        return jnp.sum(chosen * (jnp.arange(NBLK) + 1), axis=-1) - 1

    own_ids = jnp.maximum(block_ids(kept)[0], 0)
    both = jnp.concatenate([passage_k, passage_v], axis=1).reshape(NBLK, BLK, 2 * WKV)
    send = both[own_ids].reshape(ROWS, 2 * WKV)
    pieces = lax.all_gather(send, "grp", axis=0)
    local = lax.dynamic_index_in_dim(pieces, context_map[0, 0] // seqs, 0, keepdims=False)
    gathered = lax.all_gather(local, "seq", axis=0)

    ids = block_ids(all_kept[my_map])
    start = jnp.arange(seqs)[:, None] * PLEN + ids * BLK
    position = start[:, :, None] + jnp.arange(BLK)
    position = jnp.where(ids[:, :, None] >= 0, position, 2**30).reshape(seqs, 1, ROWS)
    visible = position < recompute_pos[0][None, :, None]
    bias = jnp.where(visible, 0.0, NEG).astype(jnp.float32)

    passage_out = pl.pallas_call(
        passage_kernel,
        grid=(KVH,),
        in_specs=[
            pl.BlockSpec((PLEN, GQ * HD), lambda j: (0, j)),
            pl.BlockSpec((PLEN, HD), lambda j: (0, j)),
            pl.BlockSpec((PLEN, HD), lambda j: (0, j)),
        ],
        out_specs=pl.BlockSpec((PLEN, GQ * HD), lambda j: (0, j)),
        out_shape=jax.ShapeDtypeStruct((PLEN, HQ * HD), jnp.bfloat16),
        compiler_params=pltpu.CompilerParams(vmem_limit_bytes=40 * 2**20),
        cost_estimate=pl.CostEstimate(
            flops=8 * 10**9, bytes_accessed=9 * 10**6, transcendentals=6 * 10**6
        ),
    )(passage_q, passage_k, passage_v)

    reader_out = pl.pallas_call(
        reader_kernel,
        grid=(KVH,),
        in_specs=[
            pl.BlockSpec((count, GQ * HD), lambda j: (0, j)),
            pl.BlockSpec((count, HD), lambda j: (0, j)),
            pl.BlockSpec((count, HD), lambda j: (0, j)),
            pl.BlockSpec((seqs, count, ROWS), lambda j: (0, 0, 0)),
            pl.BlockSpec((seqs, ROWS, HD), lambda j: (0, 0, j)),
            pl.BlockSpec((seqs, ROWS, HD), lambda j: (0, 0, KVH + j)),
        ],
        out_specs=pl.BlockSpec((count, GQ * HD), lambda j: (0, j)),
        out_shape=jax.ShapeDtypeStruct((count, HQ * HD), jnp.bfloat16),
        scratch_shapes=[
            pltpu.VMEM((GQ * count, HD), jnp.float32),
            pltpu.VMEM((GQ * count, 2 * HD), jnp.float32),
        ],
        compiler_params=pltpu.CompilerParams(vmem_limit_bytes=40 * 2**20),
    )(recompute_q[0], recompute_k[0], recompute_v[0], bias, gathered, gathered)
    return passage_out, reader_out[None]


def solution(mesh):
    both = P(("grp", "seq"), None)
    rows = P("grp", "seq", None)
    return jax.shard_map(
        on_device,
        mesh=mesh,
        in_specs=(both, both, both, both, P("grp", "seq"), P("grp", "seq"), rows, rows, rows),
        out_specs=(both, rows),
        check_vma=False,
    )
```

time: 220 us -> 157 us (0.71); the launches traced: 216 us -> 156 us
  matrix products: 60.5 us -> 0 us
  Pallas kernels: 0 us -> 39 us
  local copies, waits for them, and re-layouts: 39.8 us -> 9.4 us
  other arithmetic: 28.1 us -> 3.65 us
  blocking collectives: 20.6 us -> 32.7 us
  waiting for transfers between devices: 50.4 us -> 56.4 us
    dot_general x12 -> x0, matrix products: 60.5 us -> none  [the longest x1 16.6 us: encode_passage(): jnp.einsum('kgij,jkd->ikgd', weights, value_heads, preferred_element_type...]
    pallas_call x0 -> x2, Pallas kernels: none -> 39 us  [the longest x1 24.6 us: on_device(): pl.pallas_call(reader_kernel, grid=(KVH,), in_specs=[pl.BlockSpec((count,...]
    reduce_sum x4 -> x2, other arithmetic: 21.3 us -> 0.24 us  [block_ids(): return jnp.sum(chosen * (jnp.arange(NBLK) + 1), axis=-1) - 1]
    all_gather x2 -> x1, blocking collectives: 20.6 us -> 32.7 us  [on_device(): everyone = lax.all_gather(info, ('grp', 'seq'), axis=0, tiled=True)]
    dynamic_slice x8 -> x1, local copies, waits for them, and re-layouts: 11.4 us -> 2.07 us  [on_device(): lax.dynamic_index_in_dim(pieces, context_map[0, 0] // seqs, 0, keepdims=F...]
    while x6 -> x0, local copies, waits for them, and re-layouts: 9.12 us -> none
    all_gather x4 -> x2, waiting for transfers between devices: 50.3 us -> 56.4 us  [the longest x1 44.4 us: on_device(): pieces = lax.all_gather(send, 'grp', axis=0)]
    unnamed x13 -> x18, local copies, waits for them, and re-layouts: 9.9 us -> 5.02 us
  transfers between devices with their start and end apart: 4 -> 2, of which waited for: 3 -> 2; matrix products, arithmetic and copies ran while one was open for 32% -> 1% of each run, Pallas kernels for 0% -> 9%
where the time goes in v1:
time: 157 us; the launch traced here: 156 us
  waiting for transfers between devices  56.4 us (36%)
  Pallas kernels  39 us (25%)
  blocking collectives  32.7 us (21%)
  between operations  14.8 us (9%)
  local copies, waits for them, and re-layouts  9.4 us (6%)
  other arithmetic  3.65 us (2%)
    all_gather x1, waiting for transfers between devices, on_device(): pieces = lax.all_gather(send, 'grp', axis=0)  44.4 us
    all_gather x1, blocking collectives, on_device(): everyone = lax.all_gather(info, ('grp', 'seq'), axis=0, tiled=True)  32.7 us
    pallas_call x1, Pallas kernels, on_device(): pl.pallas_call(reader_kernel, grid=(KVH,), in_specs=[pl.BlockSpec((count,...  24.6 us
    pallas_call x1, Pallas kernels, on_device(): pl.pallas_call(passage_kernel, grid=(KVH,), in_specs=[pl.BlockSpec((PLEN,...  14.4 us
    all_gather x1, waiting for transfers between devices, on_device(): gathered = lax.all_gather(local, 'seq', axis=0)  12 us
    unnamed x18, local copies, waits for them, and re-layouts  5.02 us
  transfers between devices with their start and end apart: 2, of which 2 were waited for; matrix products, arithmetic and copies ran while one was open for 1% of the time, Pallas kernels for 9%

profile of v1, /device:TPU:25, one launch (start us, length us, event | category | flops | bytes accessed | tf_op | source)
XLA Modules:
  0.0 156.1 jit_solution(5610238670744268376)
XLA Ops:
  7.2 0.7 compare_bitcast_fusion
  7.9 0.8 reduce-window.7
  8.7 0.2 fusion.3
  8.9 1.3 pad_maximum_fusion
  10.3 1.5 gather_fusion.1
  11.8 0.0 all-gather.6.cloned.1.call-start
  12.5 44.4 %all-gather.4.cloned.1.call-done = bf16[4,384,1024]{2,1,0:T(8,128)(2,1)} async-done(((bf16[1,384,1024]{2,1,0:T(8,128)(2,1)}), bf16[4,384,1024]{2,1,0:T(8,128)(2,1)}) %all-gather.4.cloned.1.call-update) | async-done | bytes 3145744 | tf_op jit(solution)/shard_map/all_gather | solution.py:114
  56.9 2.1 %constant_dynamic-slice_fusion = bf16[1,384,1024]{2,1,0:T(8,128)(2,1)} fusion(bf16[4,384,1024]{2,1,0:T(8,128)(2,1)} %all-gather.4.cloned.1.call-done, s32[]{:T(128)S(6)} %select_n.34), kind=kLoop, calls=%fused_computation.26 | loop fusion | bytes 1572868 | tf_op jit(solution)/shard_map/jit(dynamic_index_in_dim)/dynamic_slice | solution.py:115
  59.0 0.1 add_bitcast_fusion
  59.1 32.7 %all-gather = s32[32,1,5]{2,1,0:T(1,128)S(1)} all-gather(s32[1,1,5]{2,1,0:T(1,128)S(1)} %add_bitcast_fusion), channel_id=1, replica_groups=mesh['grp'=4,'seq'=8] {'grp','seq'}, dimensions={0}, use_global_device_ids=true | all-gather | bytes 660 | tf_op jit(solution)/shard_map/all_gather | solution.py:101
  91.8 0.1 slice.13
  91.9 0.1 fusion.2
  92.0 0.6 gather_fusion
  92.5 0.2 reduce_window_sum.18
  92.7 0.1 copy.14
  92.8 0.1 copy.13
  92.9 0.1 select_reduce_fusion
  93.0 0.1 fusion
  93.1 0.1 compare_select_fusion.bias_ref
  93.2 2.2 %copy-done.6 = bf16[512,4096]{1,0:T(8,128)(2,1)S(1)} copy-done((bf16[512,4096]{1,0:T(8,128)(2,1)S(1)}, bf16[512,4096]{1,0:T(8,128)(2,1)}, u32[]{:S(2)}) %copy-start.6) | copy-done | bytes 4194328
  95.5 14.4 %shard_map.104 = bf16[512,4096]{1,0:T(8,128)(2,1)} custom-call(bf16[512,4096]{1,0:T(8,128)(2,1)S(1)} %copy-done.6, bf16[512,512]{1,0:T(8,128)(2,1)S(1)} %copy-done.2, bf16[512,512]{1,0:T(8,128)(2,1)S(1)} %copy-done.3), custom_call_target="tpu_custom_call" | custom-call | flops 8000000000 | bytes 9000000 | tf_op jit(solution)/shard_map/pallas_call | solution.py:125
  109.8 12.0 %all-gather.6.cloned.1.call-done.k_ref.v_ref = bf16[8,384,1024]{2,1,0:T(8,128)(2,1)} async-done(((bf16[1,384,1024]{2,1,0:T(8,128)(2,1)}), bf16[8,384,1024]{2,1,0:T(8,128)(2,1)}) %all-gather.6.cloned.1.call-update) | async-done | bytes 6291472 | tf_op jit(solution)/shard_map/all_gather | solution.py:116
  121.8 2.8 %copy-done = bf16[8,384,1024]{2,1,0:T(8,128)(2,1)S(1)} copy-done((bf16[8,384,1024]{2,1,0:T(8,128)(2,1)S(1)}, bf16[8,384,1024]{2,1,0:T(8,128)(2,1)}, u32[]{:S(2)}) %copy-start) | copy-done | bytes 6291480
  124.6 24.6 %shard_map.105 = bf16[64,4096]{1,0:T(8,128)(2,1)} custom-call(bf16[64,4096]{1,0:T(8,128)(2,1)S(1)} %bitcast.29, bf16[64,512]{1,0:T(8,128)(2,1)S(1)} %bitcast.30, bf16[64,512]{1,0:T(8,128)(2,1)S(1)} %bitcast.31, f32[8,64,384]{2,1,0:T(8,128)S(1)} %compare_select_fusion.bias_ref, bf16[8,384,1024]{2,1,0:T(8,128)(2,1)S(1)} %copy-done, ...), custom_call_target="tpu_custom_call" | custom-call | tf_op jit(solution)/shard_map/pallas_call | solution.py:141
  (30 shorter events, 0.2 us)
Async XLA Ops:
  7.2 49.7 %all-gather.4.cloned.1.call-start = ((), (), s32[]{:S(2)}) async-start(), calls=%async_computation | async-start | bytes 3932160 | tf_op jit(solution)/shard_map/all_gather | solution.py:114
  8.9 50.1 %copy-start.8 = (s32[1,4]{1,0:T(1,128)S(1)}, s32[1,4]{1,0:T(1,128)}, u32[]{:S(2)}) copy-start(s32[1,4]{1,0:T(1,128)} %param.12) | copy-start | bytes 52
  8.9 84.2 %copy-start.7 = (s32[1,64]{1,0:T(1,128)S(1)}, s32[1,64]{1,0:T(1,128)}, u32[]{:S(2)}) copy-start(s32[1,64]{1,0:T(1,128)} %param.14) | copy-start | bytes 772
  10.2 83.0 %copy-start.2 = (bf16[512,512]{1,0:T(8,128)(2,1)S(1)}, bf16[512,512]{1,0:T(8,128)(2,1)}, u32[]{:S(2)}) copy-start(bf16[512,512]{1,0:T(8,128)(2,1)} %k_ref.1) | copy-start | bytes 1572868
  10.3 83.0 %copy-start.3 = (bf16[512,512]{1,0:T(8,128)(2,1)S(1)}, bf16[512,512]{1,0:T(8,128)(2,1)}, u32[]{:S(2)}) copy-start(bf16[512,512]{1,0:T(8,128)(2,1)} %v_ref.1) | copy-start | bytes 1572868
  11.8 110.0 %all-gather.6.cloned.1.call-start = ((), (), s32[]{:S(2)}) async-start(), calls=%async_computation.1 | async-start | bytes 7077888 | tf_op jit(solution)/shard_map/all_gather | solution.py:116
  93.2 2.2 %copy-start.6 = (bf16[512,4096]{1,0:T(8,128)(2,1)S(1)}, bf16[512,4096]{1,0:T(8,128)(2,1)}, u32[]{:S(2)}) copy-start(bf16[512,4096]{1,0:T(8,128)(2,1)} %q_ref.1) | copy-start | bytes 12582916
  95.4 26.4 %copy-start.1 = (bf16[1,64,4096]{2,1,0:T(8,128)(2,1)S(1)}, bf16[1,64,4096]{2,1,0:T(8,128)(2,1)}, u32[]{:S(2)}) copy-start(bf16[1,64,4096]{2,1,0:T(8,128)(2,1)} %param.15) | copy-start | bytes 1572868
  95.4 26.4 %copy-start.4 = (bf16[1,64,512]{2,1,0:T(8,128)(2,1)S(1)}, bf16[1,64,512]{2,1,0:T(8,128)(2,1)}, u32[]{:S(2)}) copy-start(bf16[1,64,512]{2,1,0:T(8,128)(2,1)} %param.16) | copy-start | bytes 196612
  95.4 26.4 %copy-start.5 = (bf16[1,64,512]{2,1,0:T(8,128)(2,1)S(1)}, bf16[1,64,512]{2,1,0:T(8,128)(2,1)}, u32[]{:S(2)}) copy-start(bf16[1,64,512]{2,1,0:T(8,128)(2,1)} %param.17) | copy-start | bytes 196612
  121.8 2.8 %copy-start = (bf16[8,384,1024]{2,1,0:T(8,128)(2,1)S(1)}, bf16[8,384,1024]{2,1,0:T(8,128)(2,1)}, u32[]{:S(2)}) copy-start(bf16[8,384,1024]{2,1,0:T(8,128)(2,1)} %all-gather.6.cloned.1.call-done.k_ref.v_ref) | copy-start | bytes 18874372
Sparse Core Ops, SparseCore 0:
  11.9 44.9 all-gather.3
  59.1 62.6 all-gather.5

commit v2 on v1

v2 whole, which is shorter than its diff:
```python
import functools
import math

import jax
import jax.numpy as jnp
from jax import lax
from jax.experimental import pallas as pl
from jax.experimental.pallas import tpu as pltpu
from jax.sharding import PartitionSpec as P

HQ = 32
KVH = 4
HD = 128
PLEN = 512
BLK = 128
KEEP = 3
NBLK = PLEN // BLK
ROWS = KEEP * BLK
GQ = HQ // KVH
WKV = KVH * HD
CORES = 2
HKV = KVH // CORES
HALF = WKV // CORES
HALFQ = HQ * HD // CORES
QB = 256
SCALE2 = HD ** (-0.5) * math.log2(math.e)
NEG = -1e30
FAR = 2**30
MESH = pl.DeviceIdType.MESH


def dot_nt(a, b):
    return lax.dot_general(a, b, (((1,), (1,)), ((), ())), preferred_element_type=jnp.float32)


def with_ones(values):
    return jnp.concatenate([values, jnp.ones_like(values)], axis=1)


def passage_head(queries, keys, values_ones, first):
    number = first + QB
    scores = dot_nt(queries, keys[:number])
    row = lax.broadcasted_iota(jnp.int32, (QB, QB), 0)
    col = lax.broadcasted_iota(jnp.int32, (QB, QB), 1)
    diagonal = jnp.where(row >= col, scores[:, first:], NEG)
    scores = diagonal if first == 0 else jnp.concatenate([scores[:, :first], diagonal], axis=1)
    maximum = jnp.max(scores, axis=-1, keepdims=True)
    weights = jnp.exp2((scores - maximum) * SCALE2).astype(jnp.bfloat16)
    mixture = jnp.dot(weights, values_ones[:number], preferred_element_type=jnp.float32)
    return (mixture[:, :HD] / mixture[:, HD:]).astype(jnp.bfloat16)


def kept_slots(flags):
    one, two, three = (flags[i] > 0 for i in range(1, NBLK))
    first = jnp.where(one, 1, jnp.where(two, 2, jnp.where(three, 3, -1)))
    second = jnp.where(
        one, jnp.where(two, 2, jnp.where(three, 3, -1)), jnp.where(two & three, 3, -1)
    )
    return [0, first, second]


def kernel(groups, seqs, kept_s, map_s, pq, pk, pv, qpos, rq, rk, rv, pout, rout,
           send_k, send_v, pool_k, pool_v, st_k, st_v, rec_k, rec_v, kv, pos, info, info_s,
           qb, ob, okb, ovb, qpb, m_ref, acc_ref, pbuf,
           info_ss, info_rs, s1s, s1r, s2s, s2r, chs, chr_, qs, qr, qls, osem, outs, isem):
    chips = seqs // CORES
    g = lax.axis_index("grp")
    s = lax.axis_index("seq")
    z, c = s // CORES, lax.rem(s, CORES)
    other = 1 - c
    gx = g + 1 - 2 * lax.rem(g, 2)
    gy = lax.rem(g + groups // 2, groups)
    base = z * CORES
    count = rq.shape[0]

    def device(group, seq):
        return {"grp": group, "seq": seq}

    def peers():
        for step in range(1, 2 * groups):
            dg, dc = step // CORES, step % CORES
            yield step, lax.rem(g + dg, groups), base + lax.rem(c + dc, CORES)

    barrier = pltpu.get_barrier_semaphore()
    for step, pg, ps in peers():
        pl.semaphore_signal(barrier, inc=1, device_id=device(pg, ps), device_id_type=MESH)

    @pl.when(z > 0)
    def _():
        pl.semaphore_signal(barrier, inc=1, device_id=device(g, s - CORES), device_id_type=MESH)

    @pl.when(z < chips - 1)
    def _():
        pl.semaphore_signal(barrier, inc=1, device_id=device(g, s + CORES), device_id_type=MESH)

    own_slots = kept_slots([kept_s[0, i] for i in range(NBLK)])
    for slot in range(KEEP):
        index = jnp.maximum(own_slots[slot], 0)
        for source, target in ((pk, send_k), (pv, send_v)):
            block = source[index]
            for h in range(CORES):
                target[h, slot * BLK : (slot + 1) * BLK] = block[:, h * HALF : (h + 1) * HALF]
    tile_row = lax.broadcasted_iota(jnp.int32, (8, 128), 0)
    tile = jnp.full((8, 128), map_s[0, 0], jnp.int32)
    for i in range(NBLK):
        tile = jnp.where(tile_row == i, kept_s[0, i], tile)
    me8 = g * CORES + c
    info[me8] = tile
    pool_k[0, c] = send_k[c]
    pool_v[0, c] = send_v[c]

    along = jnp.minimum(z, 1) + jnp.minimum(chips - 1 - z, 1)
    pl.semaphore_wait(barrier, 2 * groups - 1 + along)

    def remote(src, dst, ssem, rsem, group, seq):
        return pltpu.make_async_remote_copy(
            src_ref=src, dst_ref=dst, send_sem=ssem, recv_sem=rsem,
            device_id=device(group, seq), device_id_type=MESH,
        )

    info_copies = []
    for step, pg, ps in peers():
        copy = remote(info.at[me8], info.at[me8], info_ss.at[step], info_rs.at[me8], pg, ps)
        copy.start()
        info_copies.append(copy)

    stage1 = []
    for index, (send, pool, first) in enumerate(((send_k, pool_k, gx), (send_v, pool_v, gy))):
        for number, (pg, pc, near) in enumerate(((first, c, 1), (first, other, 1), (g, other, 0))):
            copy = remote(send.at[pc], pool.at[near, c], s1s.at[index, number],
                          s1r.at[index, near, c], pg, base + pc)
            copy.start()
            stage1.append(copy)

    half_q = pl.ds(pl.multiple_of(c * HALFQ, HALFQ), HALFQ)
    away_q = pl.ds(pl.multiple_of(other * HALFQ, HALFQ), HALFQ)
    half_k = pl.ds(pl.multiple_of(c * HALF, HALF), HALF)
    away_k = pl.ds(pl.multiple_of(other * HALF, HALF), HALF)
    own_views = ((rq.at[:, half_q], qb), (rk.at[:, half_k], okb), (rv.at[:, half_k], ovb), (qpos, qpb))
    away_views = ((rq.at[:, away_q], qb), (rk.at[:, away_k], okb), (rv.at[:, away_k], ovb), (qpos, qpb))
    q_local, q_remote = [], []
    for index, (src, buf) in enumerate(own_views):
        copy = pltpu.make_async_copy(src, buf.at[c], qls.at[index])
        copy.start()
        q_local.append(copy)
    for index, (src, buf) in enumerate(away_views):
        copy = remote(src, buf.at[c], qs.at[index], qr.at[index], g, base + other)
        copy.start()
        q_remote.append(copy)

    out_copies = []

    def passage(j):
        keys = jnp.concatenate([pk[b, :, j * HD : (j + 1) * HD] for b in range(NBLK)], axis=0)
        values = with_ones(
            jnp.concatenate([pv[b, :, j * HD : (j + 1) * HD] for b in range(NBLK)], axis=0)
        )

        def heads(pair, carry):
            for k in range(2):
                head = j * GQ + pair * 2 + k
                cols = pl.ds(pl.multiple_of(head * HD, HD), HD)
                for first in range(0, PLEN, QB):
                    rows = slice(first, first + QB)
                    pbuf[rows, cols] = passage_head(pq[rows, cols], keys, values, first)
            return carry

        lax.fori_loop(0, GQ // 2, heads, 0)
        cols = slice(j * GQ * HD, (j + 1) * GQ * HD)
        copy = pltpu.make_async_copy(pbuf.at[:, cols], pout.at[:, cols], outs.at[j])
        copy.start()
        out_copies.append(copy)

    passage(0)
    passage(1)

    for step, pg, ps in peers():
        them = pg * CORES + lax.rem(c + step % CORES, CORES)
        remote(info.at[them], info.at[them], info_ss.at[step], info_rs.at[them], pg, ps).wait_recv()
    scalars = pltpu.make_async_copy(info, info_s, isem)
    scalars.start()
    scalars.wait()
    stage2 = []
    for index, (send, pool, st, rec, first, second) in enumerate(
        ((send_k, pool_k, st_k, rec_k, gx, gy), (send_v, pool_v, st_v, rec_v, gy, gx))
    ):
        for near, cc in ((0, other), (1, 0), (1, 1)):
            remote(send.at[0], pool.at[near, cc], s1s.at[index, 0], s1r.at[index, near, cc],
                   first, s).wait_recv()
        for cc in range(CORES):
            source = info_s[second * CORES + cc, NBLK, 0] // seqs
            st[cc] = pool[jnp.where(source == first, 1, 0), cc]
        copy = remote(st, rec, s2s.at[index], s2r.at[index], second, s)
        copy.start()
        stage2.append(copy)

    passage(2)

    for index, (pool, rec, copy, first) in enumerate(
        ((pool_k, rec_k, stage2[0], gx), (pool_v, rec_v, stage2[1], gy))
    ):
        copy.wait_recv()
        for cc in range(CORES):
            source = info_s[g * CORES + cc, NBLK, 0] // seqs
            near = pool[jnp.where(source == first, 1, 0), cc]
            here = (source == g) | (source == first)
            kv[z, index, cc * ROWS : (cc + 1) * ROWS] = jnp.where(here, near, rec[cc])
    offset = lax.broadcasted_iota(jnp.int32, (8, BLK), 1)
    for cc in range(CORES):
        wanted = info_s[g * CORES + cc, NBLK, 0] // seqs
        slots = kept_slots([info_s[wanted * CORES + cc, i, 0] for i in range(NBLK)])
        for slot in range(KEEP):
            begin = jnp.where(slots[slot] >= 0, (base + cc) * PLEN + slots[slot] * BLK, FAR)
            first_lane = cc * ROWS + slot * BLK
            pos[z, :, first_lane : first_lane + BLK] = offset + begin

    def chain(zz):
        return (
            remote(kv.at[zz], kv.at[zz], chs.at[zz, 0], chr_.at[zz, 0], g, lax.rem(s + CORES, seqs)),
            remote(pos.at[zz], pos.at[zz], chs.at[zz, 1], chr_.at[zz, 1], g, lax.rem(s + CORES, seqs)),
        )

    def forward(zz):
        @pl.when(z < chips - 1)
        def _():
            for copy in chain(zz):
                copy.start()

    forward(z)
    passage(3)

    for copy in q_local:
        copy.wait()
    for copy in q_remote:
        copy.wait()
    queries_total = CORES * count

    def head_cols(j, h):
        return slice((j * GQ + h) * HD, (j * GQ + h + 1) * HD)

    def pair_queries(j, h):
        parts = [qb[cc, :, head_cols(j, h + k)] for k in range(2) for cc in range(CORES)]
        return jnp.concatenate(parts, axis=0)

    width = 2 * queries_total
    for j in range(HKV):
        cols = slice(j * HD, (j + 1) * HD)
        own_k = jnp.concatenate([okb[0, :, cols], okb[1, :, cols]] * 2, axis=0).astype(jnp.float32)
        own_v = jnp.concatenate([ovb[0, :, cols], ovb[1, :, cols]] * 2, axis=0).astype(jnp.float32)
        for h in range(0, GQ, 2):
            rows = slice(h * queries_total, h * queries_total + width)
            product = pair_queries(j, h).astype(jnp.float32) * own_k
            score = jnp.sum(product, axis=-1, keepdims=True)
            m_ref[j, rows] = jnp.broadcast_to(score, (width, HD))
            acc_ref[j, rows, :HD] = own_v
            acc_ref[j, rows, HD:] = jnp.ones((width, HD), jnp.float32)

    def absorb(zz):
        keys_pos = pos[zz, 0:1, :]
        query_pos = jnp.concatenate([qpb[0, :, 0:1], qpb[1, :, 0:1]], axis=0)
        bias = jnp.where(keys_pos < query_pos, 0.0, NEG).astype(jnp.float32)
        bias = jnp.concatenate([bias, bias], axis=0)
        for j in range(HKV):
            cols = slice(j * HD, (j + 1) * HD)
            keys = kv[zz, 0, :, cols]
            values = with_ones(kv[zz, 1, :, cols])
            for h in range(0, GQ, 2):
                rows = slice(h * queries_total, h * queries_total + width)
                scores = dot_nt(pair_queries(j, h), keys) + bias
                old = m_ref[j, rows]
                new = jnp.maximum(old, jnp.max(scores, axis=-1, keepdims=True))
                factor = jnp.exp2((old - new) * SCALE2)
                tiled = jnp.concatenate([new] * (CORES * KEEP), axis=1)
                weights = jnp.exp2((scores - tiled) * SCALE2).astype(jnp.bfloat16)
                mixture = jnp.dot(weights, values, preferred_element_type=jnp.float32)
                acc_ref[j, rows] = acc_ref[j, rows] * jnp.concatenate([factor, factor], axis=1) + mixture
                m_ref[j, rows] = new

    def visit(k, carry):
        zz = z - k

        @pl.when(k > 0)
        def _():
            for copy in chain(zz):
                copy.wait_recv()
            forward(zz)

        absorb(zz)
        return carry

    lax.fori_loop(0, z + 1, visit, 0)

    for j in range(HKV):
        for h in range(0, GQ, 2):
            rows = slice(h * queries_total, h * queries_total + width)
            result = (acc_ref[j, rows, :HD] / acc_ref[j, rows, HD:]).astype(jnp.bfloat16)
            for k in range(2):
                for cc in range(CORES):
                    first = k * queries_total + cc * count
                    ob[cc, :, head_cols(j, h + k)] = result[first : first + count]
    swap = remote(ob.at[other], ob.at[2], osem.at[0], osem.at[1], g, base + other)
    swap.start()
    mine = pltpu.make_async_copy(ob.at[c], rout.at[:, half_q], osem.at[2])
    mine.start()
    swap.wait_recv()
    theirs = pltpu.make_async_copy(ob.at[2], rout.at[:, away_q], osem.at[3])
    theirs.start()
    mine.wait()
    theirs.wait()
    swap.wait_send()

    for copy in out_copies:
        copy.wait()
    for copy in info_copies + stage1 + stage2:
        copy.wait_send()

    @pl.when(z < chips - 1)
    def _():
        def drain(zz, carry):
            for copy in chain(zz):
                copy.wait_send()
            return carry

        lax.fori_loop(0, z + 1, drain, 0)


def on_device(groups, seqs, passage_q, passage_k, passage_v, kept, context_map, recompute_pos,
              recompute_q, recompute_k, recompute_v):
    count = recompute_q.shape[1]
    chips = seqs // CORES
    bf, f32, i32 = jnp.bfloat16, jnp.float32, jnp.int32
    dma = pltpu.SemaphoreType.DMA
    query_pos = jnp.broadcast_to(recompute_pos[0][:, None], (count, HD))
    smem = pl.BlockSpec(memory_space=pltpu.SMEM)
    vmem = pl.BlockSpec(memory_space=pltpu.VMEM)
    hbm = pl.BlockSpec(memory_space=pl.ANY)
    half = (CORES, ROWS, HALF)
    heads_rows = GQ * CORES * count
    passage_out, reader_out = pl.pallas_call(
        functools.partial(kernel, groups, seqs),
        out_shape=(
            jax.ShapeDtypeStruct((PLEN, HQ * HD), bf),
            jax.ShapeDtypeStruct((count, HQ * HD), bf),
        ),
        in_specs=[smem, smem, vmem, vmem, vmem, vmem, hbm, hbm, hbm],
        out_specs=(hbm, hbm),
        scratch_shapes=[
            pltpu.VMEM(half, bf), pltpu.VMEM(half, bf),
            pltpu.VMEM((2,) + half, bf), pltpu.VMEM((2,) + half, bf),
            pltpu.VMEM(half, bf), pltpu.VMEM(half, bf),
            pltpu.VMEM(half, bf), pltpu.VMEM(half, bf),
            pltpu.VMEM((chips, 2, CORES * ROWS, HALF), bf),
            pltpu.VMEM((chips, 8, CORES * ROWS), i32),
            pltpu.VMEM((groups * CORES, 8, 128), i32),
            pltpu.SMEM((groups * CORES, 8, 128), i32),
            pltpu.VMEM((CORES, count, HALFQ), bf),
            pltpu.VMEM((CORES + 1, count, HALFQ), bf),
            pltpu.VMEM((CORES, count, HALF), bf),
            pltpu.VMEM((CORES, count, HALF), bf),
            pltpu.VMEM((CORES, count, HD), i32),
            pltpu.VMEM((HKV, heads_rows, HD), f32),
            pltpu.VMEM((HKV, heads_rows, 2 * HD), f32),
            pltpu.VMEM((PLEN, HQ * HD), bf),
            dma((2 * groups,)), dma((2 * groups,)),
            dma((2, 3)), dma((2, 2, CORES)),
            dma((2,)), dma((2,)),
            dma((chips, 2)), dma((chips, 2)),
            dma((4,)), dma((4,)), dma((4,)), dma((4,)), dma((KVH,)), dma,
        ],
        compiler_params=pltpu.CompilerParams(
            collective_id=0, has_side_effects=True, vmem_limit_bytes=56 * 2**20
        ),
        cost_estimate=pl.CostEstimate(
            flops=16 * 10**9, bytes_accessed=12 * 10**6, transcendentals=12 * 10**6
        ),
    )(
        kept, context_map, passage_q,
        passage_k.reshape(NBLK, BLK, WKV), passage_v.reshape(NBLK, BLK, WKV),
        query_pos, recompute_q[0], recompute_k[0], recompute_v[0],
    )
    return passage_out, reader_out[None]


def solution(mesh):
    both = P(("grp", "seq"), None)
    rows = P("grp", "seq", None)
    return jax.shard_map(
        functools.partial(on_device, mesh.shape["grp"], mesh.shape["seq"]),
        mesh=mesh,
        in_specs=(both, both, both, both, P("grp", "seq"), P("grp", "seq"), rows, rows, rows),
        out_specs=(both, rows),
        check_vma=False,
    )
```

time: 157 us -> 93.7 us (0.60)
  waiting for transfers between devices: 56.4 us -> 0 us
  Pallas kernels: 39 us -> 85.3 us
  blocking collectives: 32.7 us -> 0 us
  between operations: 14.8 us -> 1.29 us
  other arithmetic: 3.65 us -> 0 us
  local copies, waits for them, and re-layouts: 9.4 us -> 6.9 us
    all_gather x2 -> x0, waiting for transfers between devices: 56.4 us -> none  [the longest x1 44.4 us: on_device(): pieces = lax.all_gather(send, 'grp', axis=0)]
    pallas_call x2 -> x1, Pallas kernels: 39 us -> 85.3 us  [on_device(): pl.pallas_call(functools.partial(kernel, groups, seqs), out_shape=(jax.Sh...]
    all_gather x1 -> x0, blocking collectives: 32.7 us -> none  [on_device(): everyone = lax.all_gather(info, ('grp', 'seq'), axis=0, tiled=True)]
    dynamic_slice x1 -> x0, local copies, waits for them, and re-layouts: 2.07 us -> none  [on_device(): lax.dynamic_index_in_dim(pieces, context_map[0, 0] // seqs, 0, keepdims=F...]
    gather x2 -> x0, local copies, waits for them, and re-layouts: 2.06 us -> none  [the longest x1 1.5 us: on_device(): send = both[own_ids].reshape(ROWS, 2 * WKV)]
    unnamed x18 -> x4, local copies, waits for them, and re-layouts: 5.02 us -> 5.55 us
  transfers between devices with their start and end apart: 2 -> 0, of which waited for: 2 -> 0; matrix products, arithmetic and copies ran while one was open for 1% -> 0% of each run, Pallas kernels for 9% -> 0%
where the time goes in v2:
time: 93.7 us; the launch traced here: 93.5 us
  Pallas kernels  85.3 us (91%)
  local copies, waits for them, and re-layouts  6.9 us (7%)
  between operations  1.29 us (1%)
    pallas_call x1, Pallas kernels, on_device(): pl.pallas_call(functools.partial(kernel, groups, seqs), out_shape=(jax.Sh...  85.3 us
    unnamed x4, local copies, waits for them, and re-layouts  5.55 us

profile of v2, /device:TPU:25, one launch (start us, length us, event | category | flops | bytes accessed | tf_op | source)
XLA Modules:
  0.0 93.5 jit_solution(14909093338683831044)
XLA Ops:
  1.3 1.3 %broadcast_in_dim.11.qpos = s32[64,128]{1,0:T(8,128)} broadcast(s32[64]{0:T(128)} %bitcast.8), dimensions={0} | broadcast | bytes 33024 | tf_op jit(solution)/shard_map/broadcast_in_dim | solution.py:333
  2.6 85.3 %shard_map.104 = (bf16[512,4096]{1,0:T(8,128)(2,1)}, bf16[64,4096]{1,0:T(8,128)(2,1)}) custom-call(s32[1,4]{1,0:T(1,128)} %kept_s.1, s32[1,1]{1,0:T(1,128)S(6)} %copy.13.map_s, bf16[512,4096]{1,0:T(8,128)(2,1)} %pq.1, bf16[4,128,512]{2,1,0:T(8,128)(2,1)} %bitcast.9, bf16[4,128,512]{2,1,0:T(8,128)(2,1)} %bitcast.10, s32[64,128]{1,0:T(8,128)} %broadcast_in_dim.11.qpos, ...), custom_call_target="tpu_custom_call" | custom-call | flops 16000000000 | bytes 12000000 | tf_op jit(solution)/shard_map/pallas_call | solution.py:339
  88.0 0.0 copy-start
  88.0 4.8 %copy.14 = bf16[512,4096]{1,0:T(8,128)(2,1)} copy(bf16[512,4096]{1,0:T(8,128)(2,1)} %get-tuple-element.8) | data formatting | bytes 8388608
  92.7 0.0 copy-done
  92.7 0.8 copy.15
Async XLA Ops:
  88.0 4.8 %copy-start = (bf16[64,4096]{1,0:T(8,128)(2,1)S(1)}, bf16[64,4096]{1,0:T(8,128)(2,1)}, u32[]{:S(2)}) copy-start(bf16[64,4096]{1,0:T(8,128)(2,1)} %get-tuple-element.5) | copy-start | bytes 1572868

commit v3 on v2

--- a/solution.py
+++ b/solution.py
@@ -59,10 +59,10 @@
     return [0, first, second]
 
 
-def kernel(groups, seqs, kept_s, map_s, pq, pk, pv, qpos, rq, rk, rv, pout, rout,
-           send_k, send_v, pool_k, pool_v, st_k, st_v, rec_k, rec_v, kv, pos, info, info_s,
+def kernel(groups, seqs, kept_s, map_s, qpos_s, pq, pk, pv, rq, rk, rv, pout, rout,
+           kv, pos, info, info_s,
            qb, ob, okb, ovb, qpb, m_ref, acc_ref, pbuf,
-           info_ss, info_rs, s1s, s1r, s2s, s2r, chs, chr_, qs, qr, qls, osem, outs, isem):
+           info_ss, info_rs, s1s, s1r, s2s, s2r, chs, chr_, qs, qr, qls, osem, outs, isem, *stages):
     chips = seqs // CORES
     g = lax.axis_index("grp")
     s = lax.axis_index("seq")
@@ -72,6 +72,11 @@
     gy = lax.rem(g + groups // 2, groups)
     base = z * CORES
     count = rq.shape[0]
+    send, pool, staged, got = (
+        [[stages[kind * 2 * HKV + index * HKV + j] for j in range(HKV)] for index in range(2)]
+        for kind in range(4)
+    )
+    axes = ((gx, gy), (gy, gx))
 
     def device(group, seq):
         return {"grp": group, "seq": seq}
@@ -96,18 +101,23 @@
     own_slots = kept_slots([kept_s[0, i] for i in range(NBLK)])
     for slot in range(KEEP):
         index = jnp.maximum(own_slots[slot], 0)
-        for source, target in ((pk, send_k), (pv, send_v)):
+        for source, target in ((pk, send[0]), (pv, send[1])):
             block = source[index]
             for h in range(CORES):
-                target[h, slot * BLK : (slot + 1) * BLK] = block[:, h * HALF : (h + 1) * HALF]
+                for j in range(HKV):
+                    first = h * HALF + j * HD
+                    target[j][h, slot * BLK : (slot + 1) * BLK] = block[:, first : first + HD]
     tile_row = lax.broadcasted_iota(jnp.int32, (8, 128), 0)
     tile = jnp.full((8, 128), map_s[0, 0], jnp.int32)
     for i in range(NBLK):
         tile = jnp.where(tile_row == i, kept_s[0, i], tile)
     me8 = g * CORES + c
     info[me8] = tile
-    pool_k[0, c] = send_k[c]
-    pool_v[0, c] = send_v[c]
+    for index in range(2):
+        for j in range(HKV):
+            pool[index][j][0, c] = send[index][j][c]
+    for i in range(count):
+        qpb[c, i : i + 1, :] = jnp.full((1, HD), qpos_s[0, i], jnp.int32)
 
     along = jnp.minimum(z, 1) + jnp.minimum(chips - 1 - z, 1)
     pl.semaphore_wait(barrier, 2 * groups - 1 + along)
@@ -124,20 +134,38 @@
         copy.start()
         info_copies.append(copy)
 
-    stage1 = []
-    for index, (send, pool, first) in enumerate(((send_k, pool_k, gx), (send_v, pool_v, gy))):
-        for number, (pg, pc, near) in enumerate(((first, c, 1), (first, other, 1), (g, other, 0))):
-            copy = remote(send.at[pc], pool.at[near, c], s1s.at[index, number],
-                          s1r.at[index, near, c], pg, base + pc)
+    stage1, stage2 = [], []
+
+    def start_first(j):
+        for index in range(2):
+            first = axes[index][0]
+            for number, (pg, pc, near) in enumerate(((first, c, 1), (first, other, 1), (g, other, 0))):
+                copy = remote(send[index][j].at[pc], pool[index][j].at[near, c],
+                              s1s.at[j, index, number], s1r.at[j, index, near, c], pg, base + pc)
+                copy.start()
+                stage1.append(copy)
+
+    def start_second(j):
+        for index in range(2):
+            first, second = axes[index]
+            for near, cc in ((0, other), (1, 0), (1, 1)):
+                remote(send[index][j].at[0], pool[index][j].at[near, cc], s1s.at[j, index, 0],
+                       s1r.at[j, index, near, cc], first, s).wait_recv()
+            for cc in range(CORES):
+                source = info_s[second * CORES + cc, NBLK, 0] // seqs
+                staged[index][j][cc] = pool[index][j][jnp.where(source == first, 1, 0), cc]
+            copy = remote(staged[index][j], got[index][j], s2s.at[j, index], s2r.at[j, index], second, s)
             copy.start()
-            stage1.append(copy)
+            stage2.append(copy)
+
+    start_first(0)
 
     half_q = pl.ds(pl.multiple_of(c * HALFQ, HALFQ), HALFQ)
     away_q = pl.ds(pl.multiple_of(other * HALFQ, HALFQ), HALFQ)
     half_k = pl.ds(pl.multiple_of(c * HALF, HALF), HALF)
     away_k = pl.ds(pl.multiple_of(other * HALF, HALF), HALF)
-    own_views = ((rq.at[:, half_q], qb), (rk.at[:, half_k], okb), (rv.at[:, half_k], ovb), (qpos, qpb))
-    away_views = ((rq.at[:, away_q], qb), (rk.at[:, away_k], okb), (rv.at[:, away_k], ovb), (qpos, qpb))
+    own_views = ((rq.at[:, half_q], qb), (rk.at[:, half_k], okb), (rv.at[:, half_k], ovb))
+    away_views = ((rq.at[:, away_q], qb), (rk.at[:, away_k], okb), (rv.at[:, away_k], ovb), (qpb.at[c], qpb))
     q_local, q_remote = [], []
     for index, (src, buf) in enumerate(own_views):
         copy = pltpu.make_async_copy(src, buf.at[c], qls.at[index])
@@ -172,7 +200,6 @@
         out_copies.append(copy)
 
     passage(0)
-    passage(1)
 
     for step, pg, ps in peers():
         them = pg * CORES + lax.rem(c + step % CORES, CORES)
@@ -180,31 +207,8 @@
     scalars = pltpu.make_async_copy(info, info_s, isem)
     scalars.start()
     scalars.wait()
-    stage2 = []
-    for index, (send, pool, st, rec, first, second) in enumerate(
-        ((send_k, pool_k, st_k, rec_k, gx, gy), (send_v, pool_v, st_v, rec_v, gy, gx))
-    ):
-        for near, cc in ((0, other), (1, 0), (1, 1)):
-            remote(send.at[0], pool.at[near, cc], s1s.at[index, 0], s1r.at[index, near, cc],
-                   first, s).wait_recv()
-        for cc in range(CORES):
-            source = info_s[second * CORES + cc, NBLK, 0] // seqs
-            st[cc] = pool[jnp.where(source == first, 1, 0), cc]
-        copy = remote(st, rec, s2s.at[index], s2r.at[index], second, s)
-        copy.start()
-        stage2.append(copy)
-
-    passage(2)
-
-    for index, (pool, rec, copy, first) in enumerate(
-        ((pool_k, rec_k, stage2[0], gx), (pool_v, rec_v, stage2[1], gy))
-    ):
-        copy.wait_recv()
-        for cc in range(CORES):
-            source = info_s[g * CORES + cc, NBLK, 0] // seqs
-            near = pool[jnp.where(source == first, 1, 0), cc]
-            here = (source == g) | (source == first)
-            kv[z, index, cc * ROWS : (cc + 1) * ROWS] = jnp.where(here, near, rec[cc])
+    start_second(0)
+    start_first(1)
     offset = lax.broadcasted_iota(jnp.int32, (8, BLK), 1)
     for cc in range(CORES):
         wanted = info_s[g * CORES + cc, NBLK, 0] // seqs
@@ -214,19 +218,35 @@
             first_lane = cc * ROWS + slot * BLK
             pos[z, :, first_lane : first_lane + BLK] = offset + begin
 
-    def chain(zz):
-        return (
-            remote(kv.at[zz], kv.at[zz], chs.at[zz, 0], chr_.at[zz, 0], g, lax.rem(s + CORES, seqs)),
-            remote(pos.at[zz], pos.at[zz], chs.at[zz, 1], chr_.at[zz, 1], g, lax.rem(s + CORES, seqs)),
-        )
-
-    def forward(zz):
+    def chain(zz, j):
+        up = lax.rem(s + CORES, seqs)
+        copies = [remote(kv.at[zz, j], kv.at[zz, j], chs.at[zz, j], chr_.at[zz, j], g, up)]
+        if j == 0:
+            copies.append(remote(pos.at[zz], pos.at[zz], chs.at[zz, HKV], chr_.at[zz, HKV], g, up))
+        return copies
+
+    def forward(zz, j):
         @pl.when(z < chips - 1)
         def _():
-            for copy in chain(zz):
+            for copy in chain(zz, j):
                 copy.start()
 
-    forward(z)
+    def finish_stage(j):
+        for index in range(2):
+            first = axes[index][0]
+            stage2[2 * j + index].wait_recv()
+            for cc in range(CORES):
+                source = info_s[g * CORES + cc, NBLK, 0] // seqs
+                near = pool[index][j][jnp.where(source == first, 1, 0), cc]
+                here = (source == g) | (source == first)
+                kv[z, j, index, cc * ROWS : (cc + 1) * ROWS] = jnp.where(here, near, got[index][j][cc])
+        forward(z, j)
+
+    passage(1)
+    finish_stage(0)
+    start_second(1)
+    passage(2)
+    finish_stage(1)
     passage(3)
 
     for copy in q_local:
@@ -255,37 +275,37 @@
             acc_ref[j, rows, :HD] = own_v
             acc_ref[j, rows, HD:] = jnp.ones((width, HD), jnp.float32)
 
-    def absorb(zz):
+    def absorb(zz, j):
         keys_pos = pos[zz, 0:1, :]
         query_pos = jnp.concatenate([qpb[0, :, 0:1], qpb[1, :, 0:1]], axis=0)
         bias = jnp.where(keys_pos < query_pos, 0.0, NEG).astype(jnp.float32)
         bias = jnp.concatenate([bias, bias], axis=0)
-        for j in range(HKV):
-            cols = slice(j * HD, (j + 1) * HD)
-            keys = kv[zz, 0, :, cols]
-            values = with_ones(kv[zz, 1, :, cols])
-            for h in range(0, GQ, 2):
-                rows = slice(h * queries_total, h * queries_total + width)
-                scores = dot_nt(pair_queries(j, h), keys) + bias
-                old = m_ref[j, rows]
-                new = jnp.maximum(old, jnp.max(scores, axis=-1, keepdims=True))
-                factor = jnp.exp2((old - new) * SCALE2)
-                tiled = jnp.concatenate([new] * (CORES * KEEP), axis=1)
-                weights = jnp.exp2((scores - tiled) * SCALE2).astype(jnp.bfloat16)
-                mixture = jnp.dot(weights, values, preferred_element_type=jnp.float32)
-                acc_ref[j, rows] = acc_ref[j, rows] * jnp.concatenate([factor, factor], axis=1) + mixture
-                m_ref[j, rows] = new
+        keys = kv[zz, j, 0]
+        values = with_ones(kv[zz, j, 1])
+        for h in range(0, GQ, 2):
+            rows = slice(h * queries_total, h * queries_total + width)
+            scores = dot_nt(pair_queries(j, h), keys) + bias
+            old = m_ref[j, rows]
+            new = jnp.maximum(old, jnp.max(scores, axis=-1, keepdims=True))
+            factor = jnp.exp2((old - new) * SCALE2)
+            tiled = jnp.concatenate([new] * (CORES * KEEP), axis=1)
+            weights = jnp.exp2((scores - tiled) * SCALE2).astype(jnp.bfloat16)
+            mixture = jnp.dot(weights, values, preferred_element_type=jnp.float32)
+            acc_ref[j, rows] = acc_ref[j, rows] * jnp.concatenate([factor, factor], axis=1) + mixture
+            m_ref[j, rows] = new
 
     def visit(k, carry):
         zz = z - k
 
-        @pl.when(k > 0)
-        def _():
-            for copy in chain(zz):
-                copy.wait_recv()
-            forward(zz)
-
-        absorb(zz)
+        for j in range(HKV):
+
+            @pl.when(k > 0)
+            def _():
+                for copy in chain(zz, j):
+                    copy.wait_recv()
+                forward(zz, j)
+
+            absorb(zz, j)
         return carry
 
     lax.fori_loop(0, z + 1, visit, 0)
@@ -317,8 +337,9 @@
     @pl.when(z < chips - 1)
     def _():
         def drain(zz, carry):
-            for copy in chain(zz):
-                copy.wait_send()
+            for j in range(HKV):
+                for copy in chain(zz, j):
+                    copy.wait_send()
             return carry
 
         lax.fori_loop(0, z + 1, drain, 0)
@@ -330,11 +351,10 @@
     chips = seqs // CORES
     bf, f32, i32 = jnp.bfloat16, jnp.float32, jnp.int32
     dma = pltpu.SemaphoreType.DMA
-    query_pos = jnp.broadcast_to(recompute_pos[0][:, None], (count, HD))
     smem = pl.BlockSpec(memory_space=pltpu.SMEM)
     vmem = pl.BlockSpec(memory_space=pltpu.VMEM)
     hbm = pl.BlockSpec(memory_space=pl.ANY)
-    half = (CORES, ROWS, HALF)
+    half = (CORES, ROWS, HD)
     heads_rows = GQ * CORES * count
     passage_out, reader_out = pl.pallas_call(
         functools.partial(kernel, groups, seqs),
@@ -342,14 +362,10 @@
             jax.ShapeDtypeStruct((PLEN, HQ * HD), bf),
             jax.ShapeDtypeStruct((count, HQ * HD), bf),
         ),
-        in_specs=[smem, smem, vmem, vmem, vmem, vmem, hbm, hbm, hbm],
+        in_specs=[smem, smem, smem, vmem, vmem, vmem, hbm, hbm, hbm],
         out_specs=(hbm, hbm),
         scratch_shapes=[
-            pltpu.VMEM(half, bf), pltpu.VMEM(half, bf),
-            pltpu.VMEM((2,) + half, bf), pltpu.VMEM((2,) + half, bf),
-            pltpu.VMEM(half, bf), pltpu.VMEM(half, bf),
-            pltpu.VMEM(half, bf), pltpu.VMEM(half, bf),
-            pltpu.VMEM((chips, 2, CORES * ROWS, HALF), bf),
+            pltpu.VMEM((chips, HKV, 2, CORES * ROWS, HD), bf),
             pltpu.VMEM((chips, 8, CORES * ROWS), i32),
             pltpu.VMEM((groups * CORES, 8, 128), i32),
             pltpu.SMEM((groups * CORES, 8, 128), i32),
@@ -362,11 +378,12 @@
             pltpu.VMEM((HKV, heads_rows, 2 * HD), f32),
             pltpu.VMEM((PLEN, HQ * HD), bf),
             dma((2 * groups,)), dma((2 * groups,)),
-            dma((2, 3)), dma((2, 2, CORES)),
-            dma((2,)), dma((2,)),
-            dma((chips, 2)), dma((chips, 2)),
+            dma((HKV, 2, 3)), dma((HKV, 2, 2, CORES)),
+            dma((HKV, 2)), dma((HKV, 2)),
+            dma((chips, HKV + 1)), dma((chips, HKV + 1)),
             dma((4,)), dma((4,)), dma((4,)), dma((4,)), dma((KVH,)), dma,
-        ],
+        ]
+        + [pltpu.VMEM(shape, bf) for shape in (half, (2,) + half, half, half) for _ in range(2 * HKV)],
         compiler_params=pltpu.CompilerParams(
             collective_id=0, has_side_effects=True, vmem_limit_bytes=56 * 2**20
         ),
@@ -374,9 +391,9 @@
             flops=16 * 10**9, bytes_accessed=12 * 10**6, transcendentals=12 * 10**6
         ),
     )(
-        kept, context_map, passage_q,
+        kept, context_map, recompute_pos, passage_q,
         passage_k.reshape(NBLK, BLK, WKV), passage_v.reshape(NBLK, BLK, WKV),
-        query_pos, recompute_q[0], recompute_k[0], recompute_v[0],
+        recompute_q[0], recompute_k[0], recompute_v[0],
     )
     return passage_out, reader_out[None]
 

time: 93.7 us -> 84.1 us (0.90)
  Pallas kernels: 85.3 us -> 77.1 us
  local copies, waits for them, and re-layouts: 6.9 us -> 5.55 us
    pallas_call x1, Pallas kernels: 85.3 us -> 77.1 us  [on_device(): pl.pallas_call(functools.partial(kernel, groups, seqs), out_shape=(jax.Sh...]
    broadcast_in_dim x1 -> x0, local copies, waits for them, and re-layouts: 1.34 us -> none  [on_device(): query_pos = jnp.broadcast_to(recompute_pos[0][:, None], (count, HD))]
where the time goes in v3:
time: 84.1 us; the launch traced here: 83.9 us
  Pallas kernels  77.1 us (92%)
  local copies, waits for them, and re-layouts  5.55 us (7%)
  between operations  1.29 us (2%)
    pallas_call x1, Pallas kernels, on_device(): pl.pallas_call(functools.partial(kernel, groups, seqs), out_shape=(jax.Sh...  77.1 us
    unnamed x4, local copies, waits for them, and re-layouts  5.55 us

profile of v3, /device:TPU:25, one launch (start us, length us, event | category | flops | bytes accessed | tf_op | source)
XLA Modules:
  0.0 83.9 jit_solution(13177032205230379948)
XLA Ops:
  1.3 77.1 %shard_map.104 = (bf16[512,4096]{1,0:T(8,128)(2,1)}, bf16[64,4096]{1,0:T(8,128)(2,1)}) custom-call(s32[1,4]{1,0:T(1,128)} %kept_s.1, s32[1,1]{1,0:T(1,128)S(6)} %copy.13.map_s, s32[1,64]{1,0:T(1,128)} %qpos_s.1, bf16[512,4096]{1,0:T(8,128)(2,1)} %pq.1, bf16[4,128,512]{2,1,0:T(8,128)(2,1)} %bitcast.7, bf16[4,128,512]{2,1,0:T(8,128)(2,1)} %bitcast.8, ...), custom_call_target="tpu_custom_call" | custom-call | flops 16000000000 | bytes 12000000 | tf_op jit(solution)/shard_map/pallas_call | solution.py:359
  78.4 0.0 copy-start
  78.4 4.8 %copy.14 = bf16[512,4096]{1,0:T(8,128)(2,1)} copy(bf16[512,4096]{1,0:T(8,128)(2,1)} %get-tuple-element.8) | data formatting | bytes 8388608
  83.1 0.0 copy-done
  83.1 0.8 copy.15
Async XLA Ops:
  78.4 4.8 %copy-start = (bf16[64,4096]{1,0:T(8,128)(2,1)S(1)}, bf16[64,4096]{1,0:T(8,128)(2,1)}, u32[]{:S(2)}) copy-start(bf16[64,4096]{1,0:T(8,128)(2,1)} %get-tuple-element.5) | copy-start | bytes 1572868

commit v4 on v3

--- a/solution.py
+++ b/solution.py
@@ -208,7 +208,6 @@
     scalars.start()
     scalars.wait()
     start_second(0)
-    start_first(1)
     offset = lax.broadcasted_iota(jnp.int32, (8, BLK), 1)
     for cc in range(CORES):
         wanted = info_s[g * CORES + cc, NBLK, 0] // seqs
@@ -244,10 +243,11 @@
 
     passage(1)
     finish_stage(0)
+    start_first(1)
+    passage(2)
     start_second(1)
-    passage(2)
+    passage(3)
     finish_stage(1)
-    passage(3)
 
     for copy in q_local:
         copy.wait()

time: 84.1 us -> 85.8 us (1.020)
  Pallas kernels: 77.1 us -> 78.8 us
    pallas_call x1, Pallas kernels: 77.1 us -> 78.8 us  [on_device(): pl.pallas_call(functools.partial(kernel, groups, seqs), out_shape=(jax.Sh...]
where the time goes in v4:
time: 85.8 us; the launch traced here: 85.6 us
  Pallas kernels  78.8 us (92%)
  local copies, waits for them, and re-layouts  5.55 us (6%)
  between operations  1.29 us (2%)
    pallas_call x1, Pallas kernels, on_device(): pl.pallas_call(functools.partial(kernel, groups, seqs), out_shape=(jax.Sh...  78.8 us
    unnamed x4, local copies, waits for them, and re-layouts  5.55 us

profile of v4, /device:TPU:25, one launch (start us, length us, event | category | flops | bytes accessed | tf_op | source)
XLA Modules:
  0.0 85.6 jit_solution(35018966149285333)
XLA Ops:
  1.3 78.8 %shard_map.104 = (bf16[512,4096]{1,0:T(8,128)(2,1)}, bf16[64,4096]{1,0:T(8,128)(2,1)}) custom-call(s32[1,4]{1,0:T(1,128)} %kept_s.1, s32[1,1]{1,0:T(1,128)S(6)} %copy.13.map_s, s32[1,64]{1,0:T(1,128)} %qpos_s.1, bf16[512,4096]{1,0:T(8,128)(2,1)} %pq.1, bf16[4,128,512]{2,1,0:T(8,128)(2,1)} %bitcast.7, bf16[4,128,512]{2,1,0:T(8,128)(2,1)} %bitcast.8, ...), custom_call_target="tpu_custom_call" | custom-call | flops 16000000000 | bytes 12000000 | tf_op jit(solution)/shard_map/pallas_call | solution.py:359
  80.1 0.0 copy-start
  80.1 4.8 %copy.14 = bf16[512,4096]{1,0:T(8,128)(2,1)} copy(bf16[512,4096]{1,0:T(8,128)(2,1)} %get-tuple-element.8) | data formatting | bytes 8388608
  84.8 0.0 copy-done
  84.8 0.8 copy.15
Async XLA Ops:
  80.1 4.8 %copy-start = (bf16[64,4096]{1,0:T(8,128)(2,1)S(1)}, bf16[64,4096]{1,0:T(8,128)(2,1)}, u32[]{:S(2)}) copy-start(bf16[64,4096]{1,0:T(8,128)(2,1)} %get-tuple-element.5) | copy-start | bytes 1572868
